TPU v7x, 32 devices: a whole 2x2x4 slice. The times are simulated.
32 devices in a mesh: grp: 2 (over y), row: 4 (over x, core), col: 4 (over z).
Axes of the slice: x: 2, y: 2, z: 4, core: 2. Of those that a mesh axis runs over, the one named last changes fastest.
Arguments:
- keys: bfloat16 [4, 128, 8192], P('grp', None, 'row'), parts along dimension 0, may hold values from -6 to 6
- values: bfloat16 [4, 128, 8192], P('grp', None, 'row'), parts along dimension 0, may hold values from -6 to 6
- queries: bfloat16 [4, 128, 8192], P('grp', None, 'row'), parts along dimension 0, may hold values from -6 to 6
- memory_in: bfloat16 [8192, 32768], P('row', 'col'), may hold values from -0.0625 to 0.0625
- memory_out: bfloat16 [32768, 8192], P('col', 'row'), may hold values from -0.03125 to 0.03125
- rates: float32 [4, 2], P('grp'), parts along dimension 0, may hold values from 0.5 to 3
- momentum: float32 [2], P('grp'), parts along dimension 0, may hold values from 0.05 to 0.99
- decay: float32 [4], P('grp'), parts along dimension 0, may hold values from 0.05 to 0.4
- valid: int32 [4], P('grp'), parts along dimension 0, may hold values from 64 to 128
Outputs:
- recalled: bfloat16 [4, 128, 8192], P('grp', 'col', 'row'), parts along dimension 0
There are 2 independent parts, one for each index of `grp`. A program takes and returns all parts, laid end to end along the dimension named above; an argument that names none is the same for every part. Nothing has to cross between parts.
All inputs are finite; a program needn't handle non-finite values.
Results may differ from a plain program's by a relative error of at most 0.035.
Values may be sent and summed in bfloat16 or wider, within the bound.
A program may use at most 576 MiB of HBM per device.

v0:
```python
import math

import jax
import jax.numpy as jnp
from jax import lax
from jax.sharding import PartitionSpec as P

D = 8192
HID = 32768
BLOCK = 128
NBLOCK = 2


def silu_grad(pre):
    sig = jax.nn.sigmoid(pre)
    return sig * (1.0 + pre * (1.0 - sig))


def silu_round(total):
    return jax.nn.silu(total).astype(jnp.bfloat16)


def hidden_full(partial_value, finish):
    total = lax.psum(partial_value.astype(jnp.bfloat16), "row").astype(jnp.float32)
    return (finish(total), total)


def error_full(out_part, value_rows, count):
    total = lax.psum(out_part.astype(jnp.bfloat16), "col").astype(jnp.float32)
    live = (jnp.arange(total.shape[0]) < count).astype(jnp.float32)[:, None]
    error = ((total - value_rows.astype(jnp.float32)) * live).astype(jnp.bfloat16)
    return error


def per_device(keys, values, queries, memory_in, memory_out, rates, momentum, decay, valid):
    w_in = memory_in.astype(jnp.float32)
    w_out = memory_out.astype(jnp.float32)
    b_in = memory_in
    b_out = memory_out
    mom_in = jnp.zeros(w_in.shape, jnp.float32)
    mom_out = jnp.zeros(w_out.shape, jnp.float32)
    results = []
    for block_index in range(NBLOCK):
        key_rows = keys[block_index]
        pre_part = jnp.dot(key_rows, b_in, preferred_element_type=jnp.float32)
        act, pre = hidden_full(pre_part, silu_round)
        out_part = jnp.dot(act, b_out, preferred_element_type=jnp.float32)
        error = error_full(out_part, values[block_index], valid[block_index])
        grad_out = lax.dot_general(
            act, error, (((0,), (0,)), ((), ())), preferred_element_type=jnp.float32
        )
        back_part = lax.dot_general(
            error, b_out, (((1,), (1,)), ((), ())), preferred_element_type=jnp.float32
        )

        def times_slope(total):
            return (total * silu_grad(pre)).astype(jnp.bfloat16)

        delta, unused_total = hidden_full(back_part, times_slope)
        grad_in = lax.dot_general(
            key_rows, delta, (((0,), (0,)), ((), ())), preferred_element_type=jnp.float32
        )
        step_in = rates[block_index, 0] / math.sqrt(D * BLOCK)
        step_out = rates[block_index, 1] / HID
        if block_index == 0:
            mom_in = -step_in * grad_in
            mom_out = -step_out * grad_out
        else:
            mom_in = momentum[block_index - 1] * mom_in - step_in * grad_in
            mom_out = momentum[block_index - 1] * mom_out - step_out * grad_out
        w_in = (1.0 - decay[block_index]) * w_in + mom_in
        w_out = (1.0 - decay[block_index]) * w_out + mom_out
        b_in = w_in.astype(jnp.bfloat16)
        b_out = w_out.astype(jnp.bfloat16)
        query_part = jnp.dot(queries[block_index], b_in, preferred_element_type=jnp.float32)
        query_act, unused_query = hidden_full(query_part, silu_round)
        read_part = jnp.dot(query_act, b_out, preferred_element_type=jnp.float32)
        results.append(
            lax.psum_scatter(read_part.astype(jnp.bfloat16), "col", scatter_dimension=0, tiled=True)
        )
    return jnp.stack(results, axis=0)


def solution(mesh):
    placed = (
        P("grp", None, "row"),
        P("grp", None, "row"),
        P("grp", None, "row"),
        P("row", "col"),
        P("col", "row"),
        P("grp", None),
        P("grp"),
        P("grp"),
        P("grp"),
    )
    return jax.shard_map(
        per_device, mesh=mesh, in_specs=placed, out_specs=P("grp", "col", "row"), check_vma=False
    )
```

profile of v0, /device:TPU:0, one launch (start us, length us, event | category | flops | bytes accessed | tf_op | source)
XLA Modules:
  0.0 662.9 jit_solution(2135711593773450176)
XLA Ops:
  6.5 16.6 %convolution_convert_fusion.5 = bf16[128,8192]{1,0:T(8,128)(2,1)} fusion(bf16[2048,8192]{1,0:T(8,128)(2,1)} %param.12, bf16[2,128,2048]{2,1,0:T(8,128)(2,1)} %param.9), kind=kOutput, calls=%fused_computation.14 | convolution fusion | flops 4296015872 | bytes 36175872 | tf_op jit(solution)/shard_map/dot_general | solution.py:45
  23.2 54.2 %all-reduce.9.cloned.1.call-done = bf16[128,8192]{1,0:T(8,128)(2,1)} async-done(((bf16[128,8192]{1,0:T(8,128)(2,1)}), bf16[128,8192]{1,0:T(8,128)(2,1)}) %all-reduce.9.cloned.1.call-update) | async-done | bytes 2097168 | tf_op jit(solution)/shard_map/psum | solution.py:24
  77.4 16.7 %convolution_convert_fusion.9 = bf16[128,2048]{1,0:T(8,128)(2,1)} fusion(bf16[8192,2048]{1,0:T(8,128)(2,1)} %param.13, bf16[128,8192]{1,0:T(8,128)(2,1)} %all-reduce.9.cloned.1.call-done), kind=kOutput, calls=%fused_computation.55 | convolution fusion | flops 4301520896 | bytes 36175872 | tf_op jit(solution)/shard_map/dot_general | solution.py:47
  94.1 0.2 all-reduce.13.cloned.1.call-start
  94.3 0.6 fusion.78
  94.9 0.6 compare_convert_fusion.1
  95.6 37.1 %all-reduce.11.cloned.1.call-done = bf16[128,2048]{1,0:T(8,128)(2,1)} async-done(((bf16[128,2048]{1,0:T(8,128)(2,1)}), bf16[128,2048]{1,0:T(8,128)(2,1)}) %all-reduce.11.cloned.1.call-update) | async-done | bytes 524304 | tf_op jit(solution)/shard_map/psum | solution.py:29
  132.6 17.3 %convolution_convert_fusion.4 = bf16[128,8192]{1,0:T(8,128)(2,1)} fusion(bf16[8192,2048]{1,0:T(8,128)(2,1)} %param.13, bf16[128,2048]{1,0:T(8,128)(2,1)} %all-reduce.11.cloned.1.call-done, f32[128]{0:T(128)S(1)} %compare_convert_fusion.1, bf16[2,128,2048]{2,1,0:T(8,128)(2,1)S(1)} %copy-done.1), kind=kOutput, calls=%fused_computation.13 | convolution fusion | flops 4297326592 | bytes 36700672 | tf_op jit(solution)/shard_map/dot_general | solution.py:52
  150.1 40.4 %copy.10 = bf16[2048,8192]{0,1:T(8,128)(2,1)} copy(bf16[2048,8192]{1,0:T(8,128)(2,1)} %param.12) | data formatting | bytes 67108864 | tf_op args[3]
  190.5 0.6 fusion.77
  192.4 0.6 fusion.79
  193.6 7.9 %all-reduce.13.cloned.1.call-done = bf16[128,8192]{1,0:T(8,128)(2,1)} async-done(((bf16[128,8192]{1,0:T(8,128)(2,1)}), bf16[128,8192]{1,0:T(8,128)(2,1)}) %all-reduce.13.cloned.1.call-update) | async-done | bytes 2097168 | tf_op jit(solution)/shard_map/psum | solution.py:24
  201.5 44.5 %fusion.3 = (bf16[2048,8192]{0,1:T(8,128)(2,1)}, f32[8192,2048]{1,0:T(8,128)}) fusion(bf16[2048,8192]{0,1:T(8,128)(2,1)} %copy.10, f32[]{:T(128)} %bitcast.1, f32[]{:T(128)} %bitcast, bf16[2,128,2048]{2,1,0:T(8,128)(2,1)} %param.9, bf16[128,8192]{1,0:T(8,128)(2,1)S(1)} %copy-done, bf16[128,8192]{1,0:T(8,128)(2,1)} %all-reduce.13.cloned.1.call-done), kind=kOutput, calls=%fused_computation.8 | convolution fusion | flops 4390387712 | bytes 138937344 | tf_op jit(solution)/shard_map/dot_general | solution.py:60
  246.1 23.1 %fusion.5 = bf16[128,8192]{1,0:T(8,128)(2,1)} fusion(bf16[2048,8192]{0,1:T(8,128)(2,1)} %get-tuple-element.15, bf16[2,128,2048]{2,1,0:T(8,128)(2,1)} %param.9), kind=kOutput, calls=%fused_computation.16 | convolution fusion | flops 4296015872 | bytes 36175872 | tf_op jit(solution)/shard_map/dot_general | solution.py:45
  269.1 0.3 all-reduce.17.cloned.1.call-start
  269.4 45.0 %fusion.2 = (bf16[8192,2048]{1,0:T(8,128)(2,1)}, f32[8192,2048]{1,0:T(8,128)}) fusion(bf16[8192,2048]{1,0:T(8,128)(2,1)} %param.13, f32[]{:T(128)} %bitcast.8, f32[]{:T(128)} %bitcast, bf16[128,2048]{1,0:T(8,128)(2,1)} %all-reduce.11.cloned.1.call-done, f32[128]{0:T(128)S(1)} %compare_convert_fusion.1, bf16[2,128,2048]{2,1,0:T(8,128)(2,1)S(1)} %copy-done.1, ...), kind=kOutput, calls=%fused_computation.7 | convolution fusion | flops 4386455552 | bytes 137363968 | tf_op jit(solution)/shard_map/dot_general | solution.py:49
  314.4 6.3 all-reduce.15.cloned.1.call-done
  320.7 16.7 %convolution_convert_fusion.7 = bf16[128,2048]{1,0:T(8,128)(2,1)} fusion(bf16[8192,2048]{1,0:T(8,128)(2,1)} %get-tuple-element.17, bf16[128,8192]{1,0:T(8,128)(2,1)} %all-reduce.15.cloned.1.call-done), kind=kOutput, calls=%fused_computation.53 | convolution fusion | flops 4301520896 | bytes 36175872 | tf_op jit(solution)/shard_map/dot_general | solution.py:47
  339.3 0.6 compare_convert_fusion
  340.0 36.0 %all-reduce.17.cloned.1.call-done = bf16[128,2048]{1,0:T(8,128)(2,1)} async-done(((bf16[128,2048]{1,0:T(8,128)(2,1)}), bf16[128,2048]{1,0:T(8,128)(2,1)}) %all-reduce.17.cloned.1.call-update) | async-done | bytes 524304 | tf_op jit(solution)/shard_map/psum | solution.py:29
  376.0 17.3 %convolution_convert_fusion.1 = bf16[128,8192]{1,0:T(8,128)(2,1)} fusion(bf16[8192,2048]{1,0:T(8,128)(2,1)} %get-tuple-element.17, bf16[128,2048]{1,0:T(8,128)(2,1)} %all-reduce.17.cloned.1.call-done, f32[128]{0:T(128)S(1)} %compare_convert_fusion, bf16[2,128,2048]{2,1,0:T(8,128)(2,1)S(1)} %copy-done.1), kind=kOutput, calls=%fused_computation.10 | convolution fusion | flops 4297326592 | bytes 36700672 | tf_op jit(solution)/shard_map/dot_general | solution.py:52
  393.4 0.4 all-reduce.21.cloned.1.call-start
  393.8 23.5 %fusion.4 = bf16[128,8192]{1,0:T(8,128)(2,1)} fusion(bf16[2048,8192]{0,1:T(8,128)(2,1)} %get-tuple-element.15, bf16[2,128,2048]{2,1,0:T(8,128)(2,1)} %param.11), kind=kOutput, calls=%fused_computation.15 | convolution fusion | flops 4296015872 | bytes 36175872 | tf_op jit(solution)/shard_map/dot_general | solution.py:75
  417.3 27.6 %all-reduce.19.cloned.1.call-done = bf16[128,8192]{1,0:T(8,128)(2,1)} async-done(((bf16[128,8192]{1,0:T(8,128)(2,1)}), bf16[128,8192]{1,0:T(8,128)(2,1)}) %all-reduce.19.cloned.1.call-update) | async-done | bytes 2097168 | tf_op jit(solution)/shard_map/psum | solution.py:24
  444.9 40.0 %fusion.6 = bf16[128,8192]{1,0:T(8,128)(2,1)} fusion(bf16[2048,8192]{0,1:T(8,128)(2,1)} %copy.10, f32[8192,2048]{1,0:T(8,128)} %get-tuple-element.16, f32[]{:T(128)} %bitcast.12, f32[]{:T(128)} %bitcast.85, f32[]{:T(128)} %bitcast.10, f32[]{:T(128)} %bitcast.1, f32[]{:T(128)} %bitcast, bf16[128,8192]{1,0:T(8,128)(2,1)} %all-reduce.15.cloned.1.call-done, ...), kind=kOutput, calls=%fused_computation.17 | convolution fusion | flops 8770289664 | bytes 108005888 | tf_op jit(solution)/shard_map/dot_general | solution.py:75
  485.7 85.2 %all-reduce.21.cloned.1.call-done = (bf16[128,8192]{1,0:T(8,128)(2,1)}, bf16[128,8192]{1,0:T(8,128)(2,1)}) async-done(((bf16[128,8192]{1,0:T(8,128)(2,1)}, bf16[128,8192]{1,0:T(8,128)(2,1)}), (bf16[128,8192]{1,0:T(8,128)(2,1)}, bf16[128,8192]{1,0:T(8,128)(2,1)})) %all-reduce.21.cloned.1.call-update) | async-done | bytes 4194320 | tf_op jit(solution)/shard_map/psum | solution.py:24
  570.9 39.2 %convolution_convert_fusion.6 = bf16[128,2048]{1,0:T(8,128)(2,1)} fusion(bf16[128,8192]{1,0:T(8,128)(2,1)} %get-tuple-element.5, bf16[8192,2048]{1,0:T(8,128)(2,1)} %param.13, f32[8192,2048]{1,0:T(8,128)} %get-tuple-element.18, f32[]{:T(128)} %bitcast.20, f32[]{:T(128)} %bitcast.86, f32[]{:T(128)} %bitcast.10, f32[]{:T(128)} %bitcast.8, f32[]{:T(128)} %bitcast, ...), kind=kOutput, calls=%fused_computation.52 | convolution fusion | flops 8771862528 | bytes 106430992 | tf_op jit(solution)/shard_map/dot_general | solution.py:77
  610.1 0.3 reduce-scatter.3.cloned.1.call-start
  610.4 16.8 %convolution_convert_fusion.8 = bf16[128,2048]{1,0:T(8,128)(2,1)} fusion(bf16[8192,2048]{1,0:T(8,128)(2,1)} %get-tuple-element.17, bf16[128,8192]{1,0:T(8,128)(2,1)} %get-tuple-element.6), kind=kOutput, calls=%fused_computation.54 | convolution fusion | flops 4301520896 | bytes 36175872 | tf_op jit(solution)/shard_map/dot_general | solution.py:77
  627.2 4.9 reduce-scatter.5.cloned.1.call-done
  632.1 22.3 %reduce-scatter.3.cloned.1.call-done = bf16[32,2048]{1,0:T(8,128)(2,1)} async-done(((bf16[128,2048]{1,0:T(8,128)(2,1)}), bf16[32,2048]{1,0:T(8,128)(2,1)}) %reduce-scatter.3.cloned.1.call-update) | async-done | bytes 131088 | tf_op jit(solution)/shard_map/reduce_scatter | solution.py:79
  654.4 1.7 pad_maximum_fusion
  (28 shorter events, 0.4 us)
Async XLA Ops:
  6.5 70.8 %all-reduce.9.cloned.1.call-start = ((), (), s32[]{:S(2)}) async-start(), calls=%async_computation.2 | async-start | bytes 4194304 | tf_op jit(solution)/shard_map/psum | solution.py:24
  23.1 71.2 %copy-start.5 = (s32[2]{0:T(128)S(1)}, s32[2]{0:T(128)}, u32[]{:S(2)}) copy-start(s32[2]{0:T(128)} %param.17) | copy-start | bytes 28
  23.1 109.5 %copy-start.1 = (bf16[2,128,2048]{2,1,0:T(8,128)(2,1)S(1)}, bf16[2,128,2048]{2,1,0:T(8,128)(2,1)}, u32[]{:S(2)}) copy-start(bf16[2,128,2048]{2,1,0:T(8,128)(2,1)} %param.10) | copy-start | bytes 3145732
  23.2 109.5 %all-reduce.11.cloned.1.call-start = ((), (), s32[]{:S(2)}) async-start(), calls=%async_computation.3 | async-start | bytes 1048576 | tf_op jit(solution)/shard_map/psum | solution.py:29
  94.1 107.5 %all-reduce.13.cloned.1.call-start = ((), (), s32[]{:S(2)}) async-start(), calls=%async_computation.4 | async-start | bytes 4194304 | tf_op jit(solution)/shard_map/psum | solution.py:24
  150.0 40.5 %copy-start.4 = (f32[2,2]{1,0:T(2,128)S(1)}, f32[2,2]{1,0:T(2,128)}, u32[]{:S(2)}) copy-start(f32[2,2]{1,0:T(2,128)} %param.14) | copy-start | bytes 52
  150.0 42.4 %copy-start.6 = (f32[2]{0:T(128)S(1)}, f32[2]{0:T(128)}, u32[]{:S(2)}) copy-start(f32[2]{0:T(128)} %param.16) | copy-start | bytes 28
  150.0 51.5 %copy-start = (bf16[128,8192]{1,0:T(8,128)(2,1)S(1)}, bf16[128,8192]{1,0:T(8,128)(2,1)}, u32[]{:S(2)}) copy-start(bf16[128,8192]{1,0:T(8,128)(2,1)} %all-reduce.9.cloned.1.call-done) | copy-start | bytes 6291460
  150.0 170.7 %all-reduce.15.cloned.1.call-start = ((), (), s32[]{:S(2)}) async-start(), calls=%async_computation.6 | async-start | bytes 4194304 | tf_op jit(solution)/shard_map/psum | solution.py:24
  269.1 106.9 %all-reduce.17.cloned.1.call-start = ((), (), s32[]{:S(2)}) async-start(), calls=%async_computation.7 | async-start | bytes 1048576 | tf_op jit(solution)/shard_map/psum | solution.py:29
  337.5 107.4 %all-reduce.19.cloned.1.call-start = ((), (), s32[]{:S(2)}) async-start(), calls=%async_computation.8 | async-start | bytes 4194304 | tf_op jit(solution)/shard_map/psum | solution.py:24
  393.4 51.5 %copy-start.2 = (bf16[2,128,2048]{2,1,0:T(8,128)(2,1)S(1)}, bf16[2,128,2048]{2,1,0:T(8,128)(2,1)}, u32[]{:S(2)}) copy-start(bf16[2,128,2048]{2,1,0:T(8,128)(2,1)} %param.9) | copy-start | bytes 3145732
  393.4 177.5 %all-reduce.21.cloned.1.call-start = ((), (), s32[]{:S(2)}) async-start(), calls=%async_computation.10 | async-start | bytes 8388608 | tf_op jit(solution)/shard_map/psum | solution.py:24
  484.9 86.0 %copy-start.3 = (bf16[128,2048]{1,0:T(8,128)(2,1)S(1)}, bf16[128,2048]{1,0:T(8,128)(2,1)}, u32[]{:S(2)}) copy-start(bf16[128,2048]{1,0:T(8,128)(2,1)} %all-reduce.17.cloned.1.call-done) | copy-start | bytes 1572868
  484.9 147.2 %reduce-scatter.5.cloned.1.call-start = ((), (), s32[]{:S(2)}) async-start(), calls=%async_computation.9 | async-start | bytes 655360 | tf_op jit(solution)/shard_map/reduce_scatter | solution.py:79
  610.1 44.3 %reduce-scatter.3.cloned.1.call-start = ((), (), s32[]{:S(2)}) async-start(), calls=%async_computation.5 | async-start | bytes 655360 | tf_op jit(solution)/shard_map/reduce_scatter | solution.py:79
Sparse Core Ops, SparseCore 0:
  23.2 54.0 all-reduce.8
  94.2 38.3 all-reduce.10
  150.1 51.3 all-reduce.12
  269.3 51.4 all-reduce.14
  337.6 38.3 all-reduce.16
  393.5 51.3 all-reduce.18
  485.0 85.7 all-reduce.20
  610.2 21.8 reduce-scatter.4
  634.5 19.8 reduce-scatter.2
where the time goes:
time: 671 us; the launch traced here: 663 us
  matrix products  317 us (47%)
  waiting for transfers between devices  282 us (42%)
  local copies, waits for them, and re-layouts  42.3 us (6%)
  between operations  17.9 us (3%)
    psum x5, waiting for transfers between devices, hidden_full(): lax.psum(partial_value.astype(jnp.bfloat16), 'row').astype(jnp.float32)  181 us
    psum x2, waiting for transfers between devices, error_full(): total = lax.psum(out_part.astype(jnp.bfloat16), 'col').astype(jnp.float32)  73.1 us
    dot_general x2, matrix products, per_device(): jnp.dot(queries[block_index], b_in, preferred_element_type=jnp.float32)  63.5 us
    dot_general x2, matrix products, per_device(): read_part = jnp.dot(query_act, b_out, preferred_element_type=jnp.float32)  56 us
    dot_general x1, matrix products, per_device(): lax.dot_general(act, error, (((0,), (0,)), ((), ())), preferred_element_t...  45 us
    dot_general x1, matrix products, per_device(): lax.dot_general(key_rows, delta, (((0,), (0,)), ((), ())), preferred_elem...  44.5 us
    unnamed x15, local copies, waits for them, and re-layouts  40.5 us
    dot_general x2, matrix products, per_device(): pre_part = jnp.dot(key_rows, b_in, preferred_element_type=jnp.float32)  39.6 us
  transfers between devices with their start and end apart: 9, of which 9 were waited for; matrix products, arithmetic and copies ran while one was open for 19% of the time, Pallas kernels for 0%

commit v1 on v0

v1 whole, which is shorter than its diff:
```python
import math

import jax
import jax.numpy as jnp
from jax import lax
from jax.sharding import PartitionSpec as P

BF = jnp.bfloat16
F32 = jnp.float32


def silu_grad(pre):
    sig = jax.nn.sigmoid(pre)
    return sig * (1.0 + pre * (1.0 - sig))


def mm(a, b, dims=((1,), (0,))):
    return lax.dot_general(a, b, (dims, ((), ())), preferred_element_type=F32)


NT = ((1,), (1,))


def scatter_row(x):
    return lax.psum_scatter(x.astype(BF), "row", scatter_dimension=1, tiled=True).astype(F32)


def gather_row(x):
    return lax.all_gather(x, "row", axis=1, tiled=True)


def per_device(keys, values, queries, w_in, w_out, rates, momentum, decay, valid):
    n_row = lax.axis_size("row")
    n_col = lax.axis_size("col")
    tokens = keys.shape[1]
    width = keys.shape[2] * n_row
    hidden = w_in.shape[1] * n_col
    step_in = rates[:, 0] / math.sqrt(width * tokens)
    step_out = rates[:, 1] / hidden
    keep0 = 1.0 - decay[0]
    keep1 = 1.0 - decay[1]
    both = keep0 * keep1
    carry = keep1 + momentum[0]
    k0, k1, q0, q1 = keys[0], keys[1], queries[0], queries[1]

    pre0 = scatter_row(mm(k0, w_in))
    gram = jnp.stack([mm(q0, k0, NT), mm(k1, k0, NT), mm(q1, k0, NT), mm(q1, k1, NT)])
    gram = lax.psum(gram, "row")
    rest = scatter_row(mm(jnp.concatenate([k1, q0, q1], axis=0), w_in))
    sum_k1, sum_q0, sum_q1 = rest[:tokens], rest[tokens : 2 * tokens], rest[2 * tokens :]

    def corr(index, scale, delta):
        return mm((scale * gram[index]).astype(BF), delta)

    def error_of(part, block):
        total = lax.psum(part.astype(BF), "col").astype(F32)
        live = (jnp.arange(tokens) < valid[block]).astype(F32)[:, None]
        return ((total - values[block].astype(F32)) * live).astype(BF)

    act0 = gather_row(jax.nn.silu(pre0).astype(BF))
    err0 = error_of(mm(act0, w_out), 0)
    delta0 = (scatter_row(mm(err0, w_out, NT)) * silu_grad(pre0)).astype(BF)
    pre1 = keep0 * sum_k1 - corr(1, step_in[0], delta0)
    act1 = gather_row(jax.nn.silu(pre1).astype(BF))
    qpre0 = keep0 * sum_q0 - corr(0, step_in[0], delta0)
    qact0 = gather_row(jax.nn.silu(qpre0).astype(BF))
    out1 = keep0 * mm(act1, w_out) - mm((step_out[0] * mm(act1, act0, NT)).astype(BF), err0)
    err1 = error_of(out1, 1)
    read0 = keep0 * mm(qact0, w_out) - mm((step_out[0] * mm(qact0, act0, NT)).astype(BF), err0)
    res0 = lax.psum_scatter(read0.astype(BF), "col", scatter_dimension=0, tiled=True)
    back1 = keep0 * mm(err1, w_out, NT) - mm((step_out[0] * mm(err1, err0, NT)).astype(BF), act0)
    delta1 = (scatter_row(back1) * silu_grad(pre1)).astype(BF)
    qpre1 = both * sum_q1 - corr(2, carry * step_in[0], delta0) - corr(3, step_in[1], delta1)
    qact1 = gather_row(jax.nn.silu(qpre1).astype(BF))
    read1 = (
        both * mm(qact1, w_out)
        - mm((carry * step_out[0] * mm(qact1, act0, NT)).astype(BF), err0)
        - mm((step_out[1] * mm(qact1, act1, NT)).astype(BF), err1)
    )
    res1 = lax.psum_scatter(read1.astype(BF), "col", scatter_dimension=0, tiled=True)
    return jnp.stack([res0, res1], axis=0)


def solution(mesh):
    placed = (
        P("grp", None, "row"),
        P("grp", None, "row"),
        P("grp", None, "row"),
        P("row", "col"),
        P("col", "row"),
        P("grp", None),
        P("grp"),
        P("grp"),
        P("grp"),
    )
    return jax.shard_map(
        per_device, mesh=mesh, in_specs=placed, out_specs=P("grp", "col", "row"), check_vma=False
    )
```

time: 671 us -> 522 us (0.78)
  matrix products: 317 us -> 182 us
  local copies, waits for them, and re-layouts: 42.3 us -> 4.24 us
  waiting for transfers between devices: 282 us -> 297 us
  other arithmetic: 2.98 us -> 11.9 us
    psum x7 -> x3, waiting for transfers between devices: 254 us -> 82.6 us  [the longest x2 51.8 us: error_of(): total = lax.psum(part.astype(BF), 'col').astype(F32)]
    dot_general x12 -> x21, matrix products: 317 us -> 182 us  [mm(): return lax.dot_general(a, b, (dims, ((), ())), preferred_element_type=F32)]
    reduce_scatter x2 -> x6, waiting for transfers between devices: 27.2 us -> 149 us  [the longest x4 127 us: scatter_row(): lax.psum_scatter(x.astype(BF), 'row', scatter_dimension=1, tiled=True)]
    all_gather x0 -> x4, waiting for transfers between devices: none -> 65.4 us  [gather_row(): return lax.all_gather(x, 'row', axis=1, tiled=True)]
    unnamed x15 -> x16, local copies, waits for them, and re-layouts: 40.5 us -> 1.48 us
    convert_element_type x2 -> x6, other arithmetic: 1.29 us -> 9.46 us  [the longest x1 3.45 us: scatter_row(): lax.psum_scatter(x.astype(BF), 'row', scatter_dimension=1, tiled=True)]
  transfers between devices with their start and end apart: 9 -> 13, of which waited for: 9 -> 12; matrix products, arithmetic and copies ran while one was open for 19% -> 21% of each run, Pallas kernels for 0% -> 0%
where the time goes in v1:
time: 522 us; the launch traced here: 514 us
  waiting for transfers between devices  297 us (57%)
  matrix products  182 us (35%)
  between operations  17.2 us (3%)
  other arithmetic  11.9 us (2%)
    dot_general x21, matrix products, mm(): return lax.dot_general(a, b, (dims, ((), ())), preferred_element_type=F32)  182 us
    reduce_scatter x4, waiting for transfers between devices, scatter_row(): lax.psum_scatter(x.astype(BF), 'row', scatter_dimension=1, tiled=True)  127 us
    all_gather x4, waiting for transfers between devices, gather_row(): return lax.all_gather(x, 'row', axis=1, tiled=True)  65.4 us
    psum x2, waiting for transfers between devices, error_of(): total = lax.psum(part.astype(BF), 'col').astype(F32)  51.8 us
    psum x1, waiting for transfers between devices, per_device(): gram = lax.psum(gram, 'row')  30.7 us
    reduce_scatter x1, waiting for transfers between devices, per_device(): lax.psum_scatter(read1.astype(BF), 'col', scatter_dimension=0, tiled=True)  21.7 us
  transfers between devices with their start and end apart: 13, of which 12 were waited for; matrix products, arithmetic and copies ran while one was open for 21% of the time, Pallas kernels for 0%

profile of v1, /device:TPU:0, one launch (start us, length us, event | category | flops | bytes accessed | tf_op | source)
XLA Modules:
  0.0 513.9 jit_solution(15650284106531104135)
XLA Ops:
  6.5 16.6 %convolution_convert_fusion.2 = bf16[128,8192]{1,0:T(8,128)(2,1)} fusion(bf16[2048,8192]{1,0:T(8,128)(2,1)} %param.12, bf16[2,128,2048]{2,1,0:T(8,128)(2,1)} %param.9), kind=kOutput, calls=%fused_computation.5 | convolution fusion | flops 4296015872 | bytes 36175872 | tf_op jit(solution)/shard_map/dot_general | solution.py:18
  23.2 34.2 %reduce-scatter.9.cloned.1.call-done = bf16[128,2048]{1,0:T(8,128)(2,1)} async-done(((bf16[128,8192]{1,0:T(8,128)(2,1)}), bf16[128,2048]{1,0:T(8,128)(2,1)}) %reduce-scatter.9.cloned.1.call-update) | async-done | bytes 524304 | tf_op jit(solution)/shard_map/reduce_scatter | solution.py:25
  57.4 2.1 fusion.17
  60.6 21.7 %all-gather.5.cloned.1.call-done = bf16[128,8192]{1,0:T(8,128)(2,1)} async-done(((bf16[128,2048]{1,0:T(8,128)(2,1)}), bf16[128,8192]{1,0:T(8,128)(2,1)}) %all-gather.5.cloned.1.call-update) | async-done | bytes 2097168 | tf_op jit(solution)/shard_map/all_gather | solution.py:29
  82.3 16.5 %convolution_convert_fusion.3 = bf16[128,2048]{1,0:T(8,128)(2,1)} fusion(bf16[128,8192]{1,0:T(8,128)(2,1)} %all-gather.5.cloned.1.call-done, bf16[8192,2048]{1,0:T(8,128)(2,1)} %param.13), kind=kOutput, calls=%fused_computation.20 | convolution fusion | flops 4295229440 | bytes 36175872 | tf_op jit(solution)/shard_map/dot_general | solution.py:18
  99.1 21.0 %convolution_convert_fusion = bf16[384,8192]{1,0:T(8,128)(2,1)} fusion(bf16[2048,8192]{1,0:T(8,128)(2,1)} %param.12, bf16[128,2048]{1,0:T(8,128)(2,1)} %get-tuple-element.6, bf16[128,2048]{1,0:T(8,128)(2,1)S(1)} %get-tuple-element.5, bf16[128,2048]{1,0:T(8,128)(2,1)S(1)} %slice_bitcast_fusion.2), kind=kOutput, calls=%fused_computation | convolution fusion | flops 12892766208 | bytes 41418752 | tf_op jit(solution)/shard_map/dot_general | solution.py:18
  123.3 14.0 %all-reduce.6.cloned.1.call-done = bf16[128,2048]{1,0:T(8,128)(2,1)} async-done(((bf16[128,2048]{1,0:T(8,128)(2,1)}), bf16[128,2048]{1,0:T(8,128)(2,1)}) %all-reduce.6.cloned.1.call-update) | async-done | bytes 524304 | tf_op jit(solution)/shard_map/psum | solution.py:56
  138.7 19.0 %convolution_convert_fusion.1 = bf16[128,8192]{1,0:T(8,128)(2,1)} fusion(bf16[128,2048]{1,0:T(8,128)(2,1)S(1)} %fusion.25, bf16[8192,2048]{1,0:T(8,128)(2,1)} %param.13), kind=kOutput, calls=%fused_computation.4 | convolution fusion | flops 4296015872 | bytes 36175872 | tf_op jit(solution)/shard_map/dot_general | solution.py:18
  160.3 38.0 %reduce-scatter.7.cloned.1.call-done = bf16[384,2048]{1,0:T(8,128)(2,1)} async-done(((bf16[384,8192]{1,0:T(8,128)(2,1)}), bf16[384,2048]{1,0:T(8,128)(2,1)}) %reduce-scatter.7.cloned.1.call-update) | async-done | bytes 1572880 | tf_op jit(solution)/shard_map/reduce_scatter | solution.py:25
  198.2 3.5 convert_element_type.132
  201.7 30.7 %all-reduce.4.cloned.1.call-done = f32[4,128,128]{2,1,0:T(8,128)} async-done(((f32[4,128,128]{2,1,0:T(8,128)}), f32[4,128,128]{2,1,0:T(8,128)}) %all-reduce.4.cloned.1.call-update) | async-done | bytes 262160 | tf_op jit(solution)/shard_map/psum | solution.py:48
  232.4 34.0 %reduce-scatter.11.cloned.1.call-done = bf16[128,2048]{1,0:T(8,128)(2,1)} async-done(((bf16[128,8192]{1,0:T(8,128)(2,1)}), bf16[128,2048]{1,0:T(8,128)(2,1)}) %reduce-scatter.11.cloned.1.call-update) | async-done | bytes 524304 | tf_op jit(solution)/shard_map/reduce_scatter | solution.py:25
  266.4 4.1 multiply_convert_fusion.2
  270.7 22.5 %all-gather.9.cloned.1.call-done = bf16[128,8192]{1,0:T(8,128)(2,1)} async-done(((bf16[128,2048]{1,0:T(8,128)(2,1)}), bf16[128,8192]{1,0:T(8,128)(2,1)}) %all-gather.9.cloned.1.call-update) | async-done | bytes 2097168 | tf_op jit(solution)/shard_map/all_gather | solution.py:29
  293.2 16.7 %convolution_multiply_fusion.2 = f32[128,2048]{1,0:T(8,128)} fusion(bf16[128,8192]{1,0:T(8,128)(2,1)} %all-gather.9.cloned.1.call-done, bf16[8192,2048]{1,0:T(8,128)(2,1)} %param.13, f32[]{:T(128)} %bitcast), kind=kOutput, calls=%fused_computation.7 | convolution fusion | flops 4295229440 | bytes 36700164 | tf_op jit(solution)/shard_map/dot_general | solution.py:18
  309.9 4.6 fusion.2
  315.2 37.8 %all-reduce.8.cloned.1.call-done = bf16[128,2048]{1,0:T(8,128)(2,1)} async-done(((bf16[128,2048]{1,0:T(8,128)(2,1)}), bf16[128,2048]{1,0:T(8,128)(2,1)}) %all-reduce.8.cloned.1.call-update) | async-done | bytes 524304 | tf_op jit(solution)/shard_map/psum | solution.py:56
  354.4 17.6 %convolution_multiply_fusion = f32[128,8192]{1,0:T(8,128)} fusion(bf16[128,2048]{1,0:T(8,128)(2,1)S(1)} %fusion.23, bf16[8192,2048]{1,0:T(8,128)(2,1)} %param.13, f32[]{:T(128)} %bitcast), kind=kOutput, calls=%fused_computation.2 | convolution fusion | flops 4296015872 | bytes 38273028 | tf_op jit(solution)/shard_map/dot_general | solution.py:18
  372.0 5.4 %fusion = bf16[128,8192]{1,0:T(8,128)(2,1)} fusion(f32[128,8192]{1,0:T(8,128)} %convolution_multiply_fusion, bf16[128,8192]{1,0:T(8,128)(2,1)S(1)} %copy-done, bf16[128,2048]{1,0:T(8,128)(2,1)S(1)} %fusion.23, bf16[128,2048]{1,0:T(8,128)(2,1)S(1)} %fusion.25, f32[]{:T(128)} %bitcast.13), kind=kOutput, calls=%fused_computation.3 | convolution fusion | flops 337674240 | bytes 9437188 | tf_op jit(solution)/shard_map/dot_general | solution.py:18
  378.4 3.9 multiply_convert_fusion.3
  384.3 3.5 convolution_subtract_fusion.6
  387.8 21.2 %reduce-scatter.15.cloned.1.call-done = bf16[128,2048]{1,0:T(8,128)(2,1)} async-done(((bf16[128,8192]{1,0:T(8,128)(2,1)}), bf16[128,2048]{1,0:T(8,128)(2,1)}) %reduce-scatter.15.cloned.1.call-update) | async-done | bytes 524304 | tf_op jit(solution)/shard_map/reduce_scatter | solution.py:25
  409.0 3.9 multiply_convert_fusion
  413.9 19.2 %all-gather.7.cloned.1.call-done = bf16[128,8192]{1,0:T(8,128)(2,1)} async-done(((bf16[128,2048]{1,0:T(8,128)(2,1)}), bf16[128,8192]{1,0:T(8,128)(2,1)}) %all-gather.7.cloned.1.call-update) | async-done | bytes 2097168 | tf_op jit(solution)/shard_map/all_gather | solution.py:29
  433.1 17.4 %convolution_multiply_fusion.3 = f32[128,2048]{1,0:T(8,128)} fusion(bf16[128,8192]{1,0:T(8,128)(2,1)} %all-gather.7.cloned.1.call-done, bf16[8192,2048]{1,0:T(8,128)(2,1)} %param.13, f32[]{:T(128)} %bitcast), kind=kOutput, calls=%fused_computation.8 | convolution fusion | flops 4295229440 | bytes 36700164 | tf_op jit(solution)/shard_map/dot_general | solution.py:18
  450.5 4.6 fusion.1
  455.4 2.0 all-gather.11.cloned.1.call-done
  457.4 16.8 %convolution_multiply_fusion.1 = f32[128,2048]{1,0:T(8,128)} fusion(bf16[128,8192]{1,0:T(8,128)(2,1)} %all-gather.11.cloned.1.call-done, bf16[8192,2048]{1,0:T(8,128)(2,1)} %param.13, f32[]{:T(128)S(6)} %mul.156), kind=kOutput, calls=%fused_computation.6 | convolution fusion | flops 4295229440 | bytes 36700164 | tf_op jit(solution)/shard_map/dot_general | solution.py:18
  474.2 4.1 convolution_subtract_fusion.2
  478.3 5.1 fusion.3
  483.5 21.7 %reduce-scatter.17.cloned.1.call-done = bf16[32,2048]{1,0:T(8,128)(2,1)} async-done(((bf16[128,2048]{1,0:T(8,128)(2,1)}), bf16[32,2048]{1,0:T(8,128)(2,1)}) %reduce-scatter.17.cloned.1.call-update) | async-done | bytes 131088 | tf_op jit(solution)/shard_map/reduce_scatter | solution.py:80
  505.2 1.7 pad_maximum_fusion.1
  (58 shorter events, 11.8 us)
Async XLA Ops:
  6.5 50.9 %reduce-scatter.9.cloned.1.call-start = ((), (), s32[]{:S(2)}) async-start(), calls=%async_computation.8 | async-start | bytes 2621440 | tf_op jit(solution)/shard_map/reduce_scatter | solution.py:25
  23.1 36.5 %copy-start.1 = (bf16[2,128,2048]{2,1,0:T(8,128)(2,1)S(1)}, bf16[2,128,2048]{2,1,0:T(8,128)(2,1)}, u32[]{:S(2)}) copy-start(bf16[2,128,2048]{2,1,0:T(8,128)(2,1)} %param.9) | copy-start | bytes 3145732
  23.1 36.6 %copy-start.2 = (bf16[2,128,2048]{2,1,0:T(8,128)(2,1)S(1)}, bf16[2,128,2048]{2,1,0:T(8,128)(2,1)}, u32[]{:S(2)}) copy-start(bf16[2,128,2048]{2,1,0:T(8,128)(2,1)} %param.11) | copy-start | bytes 3145732
  23.1 59.2 %all-gather.5.cloned.1.call-start = ((), (), s32[]{:S(2)}) async-start(), calls=%async_computation.9 | async-start | bytes 2621440 | tf_op jit(solution)/shard_map/all_gather | solution.py:29
  59.6 77.7 %all-reduce.6.cloned.1.call-start = ((), (), s32[]{:S(2)}) async-start(), calls=%async_computation.10 | async-start | bytes 1048576 | tf_op jit(solution)/shard_map/psum | solution.py:56
  98.8 99.4 %reduce-scatter.7.cloned.1.call-start = ((), (), s32[]{:S(2)}) async-start(), calls=%async_computation.6 | async-start | bytes 7864320 | tf_op jit(solution)/shard_map/reduce_scatter | solution.py:25
  120.0 112.4 %all-reduce.4.cloned.1.call-start = ((), (), s32[]{:S(2)}) async-start(), calls=%async_computation.7 | async-start | bytes 524288 | tf_op jit(solution)/shard_map/psum | solution.py:48
  120.4 1.7 copy-start.5
  122.1 144.3 %reduce-scatter.11.cloned.1.call-start = ((), (), s32[]{:S(2)}) async-start(), calls=%async_computation.11 | async-start | bytes 2621440 | tf_op jit(solution)/shard_map/reduce_scatter | solution.py:25
  157.7 0.7 copy-start.6
  157.7 1.9 copy-start.4
  157.7 135.5 %all-gather.9.cloned.1.call-start = ((), (), s32[]{:S(2)}) async-start(), calls=%async_computation.14 | async-start | bytes 2621440 | tf_op jit(solution)/shard_map/all_gather | solution.py:29
  160.3 106.1 %copy-start.3 = (bf16[128,2048]{1,0:T(8,128)(2,1)S(1)}, bf16[128,2048]{1,0:T(8,128)(2,1)}, u32[]{:S(2)}) copy-start(bf16[128,2048]{1,0:T(8,128)(2,1)} %reduce-scatter.9.cloned.1.call-done) | copy-start | bytes 1572868
  270.5 39.4 %copy-start = (bf16[128,8192]{1,0:T(8,128)(2,1)S(1)}, bf16[128,8192]{1,0:T(8,128)(2,1)}, u32[]{:S(2)}) copy-start(bf16[128,8192]{1,0:T(8,128)(2,1)} %all-gather.5.cloned.1.call-done) | copy-start | bytes 6291460
  270.5 82.5 %all-reduce.8.cloned.1.call-start = ((), (), s32[]{:S(2)}) async-start(), calls=%async_computation.15 | async-start | bytes 1048576 | tf_op jit(solution)/shard_map/psum | solution.py:56
  314.5 94.5 %reduce-scatter.15.cloned.1.call-start = ((), (), s32[]{:S(2)}) async-start(), calls=%async_computation.16 | async-start | bytes 2621440 | tf_op jit(solution)/shard_map/reduce_scatter | solution.py:25
  377.4 0.9 copy-start.7
  377.4 55.7 %all-gather.7.cloned.1.call-start = ((), (), s32[]{:S(2)}) async-start(), calls=%async_computation.12 | async-start | bytes 2621440 | tf_op jit(solution)/shard_map/all_gather | solution.py:29
  382.2 75.2 %all-gather.11.cloned.1.call-start = ((), (), s32[]{:S(2)}) async-start(), calls=%async_computation.17 | async-start | bytes 2621440 | tf_op jit(solution)/shard_map/all_gather | solution.py:29
  412.9 70.6 %reduce-scatter.13.cloned.1.call-start = ((), (), s32[]{:S(2)}) async-start(), calls=%async_computation.13 | async-start | bytes 655360 | tf_op jit(solution)/shard_map/reduce_scatter | solution.py:70
  455.1 50.1 %reduce-scatter.17.cloned.1.call-start = ((), (), s32[]{:S(2)}) async-start(), calls=%async_computation.18 | async-start | bytes 655360 | tf_op jit(solution)/shard_map/reduce_scatter | solution.py:80
Sparse Core Ops, SparseCore 0:
  23.3 34.1 reduce-scatter.8
  59.7 22.5 all-gather.4
  99.0 38.2 all-reduce.5
  139.8 58.3 reduce-scatter.6
  200.4 31.9 all-reduce.3
  234.9 31.3 reduce-scatter.10
  270.6 22.5 all-gather.8
  314.7 38.2 all-reduce.7
  377.6 31.4 reduce-scatter.14
  410.5 22.5 all-gather.6
  434.8 22.5 all-gather.10
  459.6 21.6 reduce-scatter.12
  483.7 21.4 reduce-scatter.16
